TPU v7x, 32 devices: a whole 2x2x4 slice. The times are simulated.
32 devices in a mesh: groups: 2 (over y), gz: 4 (over z), gy: 2 (over x), gx: 2 (over core).
Axes of the slice: x: 2, y: 2, z: 4, core: 2. Of those that a mesh axis runs over, the one named last changes fastest.
Arguments:
- density: float32 [72, 20, 244], P(('groups', 'gz'), 'gy', 'gx'), parts along dimension 0, may hold values from 2 to 4
- momentum: float32 [3, 72, 20, 244], P(None, ('groups', 'gz'), 'gy', 'gx'), parts along dimension 1, may hold values from -1 to 1
- energy: float32 [72, 20, 244], P(('groups', 'gz'), 'gy', 'gx'), parts along dimension 0, may hold values from 4 to 8
- cotangent: float32 [5, 72, 20, 244], P(None, ('groups', 'gz'), 'gy', 'gx'), parts along dimension 1, may hold values from -6 to 6
- bc_codes: int32 [8], P('groups'), parts along dimension 0, may hold values from 0 to 1, as said below
- weight_in: float32 [3, 16], replicated, may hold values from -6 to 6
- weight_out: float32 [16, 3], replicated, may hold values from -6 to 6
Outputs:
- new_state: float32 [5, 72, 20, 244], P(None, ('groups', 'gz'), 'gy', 'gx'), parts along dimension 1
- state_grad: float32 [5, 72, 20, 244], P(None, ('groups', 'gz'), 'gy', 'gx'), parts along dimension 1
There are 2 independent parts, one for each index of `groups`. A program takes and returns all parts, laid end to end along the dimension named above; an argument that names none is the same for every part. Nothing has to cross between parts.
Inputs may be any that keep to these rules, and one draw needn't show every extreme that they name: `bc_codes`: 0 marks a reflecting wall, 1 a zero-gradient outflow; exactly two of the four faces are walls.
All inputs are finite; a program needn't handle non-finite values.
Results may differ from a plain program's by a relative error of at most 0.0003.
Values sent between devices are 32-bit elements; how exact they have to be, the bound alone decides.
A program may use at most 320 MiB of HBM per device.

v0:
```python
import functools
import jax
import jax.numpy as jnp
from jax import lax
from jax.experimental import pallas as pl
from jax.experimental.pallas import tpu as pltpu
from jax.sharding import PartitionSpec as P

DT = 0.06
HID = 16
CZ, CY, CX = 9, 10, 122
ROWS = 96
LANES = 128
OWN = CZ * CY
FACE_ROWS = {"z": (0, 104, 104), "y": (208, 312, 104), "x": (416, 512, 96)}
FACES = 608
CELLS = 160
GPAD = 208
PITCH = {"z": 10, "y": 9}
COMP = {"z": 3, "y": 2, "x": 1}
W_IN = 12
W_OUT = 12 + 3 * HID


def roll(v, amount):
    return pltpu.roll(v, amount % LANES, 1)


def lane_mask(rows, low, high):
    lanes = lax.broadcasted_iota(jnp.int32, (rows, LANES), 1)
    return jnp.where((lanes >= low) & (lanes < high), 1.0, 0.0).astype(jnp.float32)


def cell_terms(comp, u):
    inverse = 1.0 / u[0]
    veloc = [u[i] * inverse for i in (1, 2, 3)]
    press = 0.4 * (u[4] - 0.5 * (u[1] * veloc[0] + u[2] * veloc[1] + u[3] * veloc[2]))
    normal = veloc[comp - 1]
    flux = [u[comp]]
    for i in (1, 2, 3):
        term = u[i] * normal
        flux.append(term + press if i == comp else term)
    flux.append((u[4] + press) * normal)
    return flux, veloc + [press * inverse]


def weno_unit(d, scal, grad, want_value):
    ratios, inverses = [], []
    feats = [0.0, 0.0, 0.0]
    for c in range(5):
        d1, d2, d3, d4 = d[0][c], d[1][c], d[2][c], d[3][c]
        b0 = 4.0 * d1 * d1 + d2 * (10.0 * d2 - 11.0 * d1)
        b1 = 4.0 * d3 * d3 + d2 * (4.0 * d2 - 5.0 * d3)
        b2 = 4.0 * d4 * d4 + d3 * (10.0 * d3 - 11.0 * d4)
        inv = 1.0 / (b0 + b1 + b2 + 0.3)
        r = [b0 * inv, b1 * inv, b2 * inv]
        ratios.append(r)
        inverses.append(inv)
        feats = [feats[k] + r[k] for k in range(3)]
    feats = [0.2 * f for f in feats]
    hidden = []
    for j in range(HID):
        pre = scal[W_IN + j] * feats[0]
        pre = pre + scal[W_IN + HID + j] * feats[1]
        pre = pre + scal[W_IN + 2 * HID + j] * feats[2]
        hidden.append(jnp.tanh(pre))
    linear = (0.1, 0.6, 0.3)
    gates, slopes = [], []
    for k in range(3):
        s = scal[W_OUT + k] * hidden[0]
        for j in range(1, HID):
            s = s + scal[W_OUT + 3 * j + k] * hidden[j]
        e = jnp.exp(-jnp.abs(s))
        gates.append(linear[k] * (jnp.maximum(s, 0.0) + jnp.log(1.0 + e) + 0.05))
        if grad is not None:
            slopes.append(linear[k] * jnp.where(s >= 0.0, 1.0, e) / (1.0 + e))
    inv_sum = 1.0 / (gates[0] + gates[1] + gates[2])
    w = [g * inv_sum for g in gates]
    a = [
        w[0] * (-1.0 / 3.0),
        (5.0 * w[0] + w[1]) * (1.0 / 6.0),
        (w[1] + 2.0 * w[2]) * (1.0 / 3.0),
        w[2] * (-1.0 / 6.0),
    ]
    value = None
    if want_value:
        value = [
            a[0] * d[0][c] + a[1] * d[1][c] + a[2] * d[2][c] + a[3] * d[3][c] for c in range(5)
        ]
    if grad is None:
        return value, None
    q = []
    for i in range(4):
        t = grad[0] * d[i][0]
        for c in range(1, 5):
            t = t + grad[c] * d[i][c]
        q.append(t * (1.0 / 6.0))
    dw = [5.0 * q[1] - 2.0 * q[0], q[1] + 2.0 * q[2], 4.0 * q[2] - q[3]]
    mid = w[0] * dw[0] + w[1] * dw[1] + w[2] * dw[2]
    ds = [(dw[k] - mid) * inv_sum * slopes[k] for k in range(3)]
    e = [0.0, 0.0, 0.0]
    for j in range(HID):
        dh = scal[W_OUT + 3 * j] * ds[0]
        dh = dh + scal[W_OUT + 3 * j + 1] * ds[1]
        dh = dh + scal[W_OUT + 3 * j + 2] * ds[2]
        dpre = dh * (1.0 - hidden[j] * hidden[j])
        e = [e[k] + scal[W_IN + HID * k + j] * dpre for k in range(3)]
    e = [0.2 * v for v in e]
    cells = [[], [], [], [], []]
    for c in range(5):
        d1, d2, d3, d4 = d[0][c], d[1][c], d[2][c], d[3][c]
        r, inv, gc = ratios[c], inverses[c], grad[c]
        m = e[0] * r[0] + e[1] * r[1] + e[2] * r[2]
        g0, g1, g2 = (e[0] - m) * inv, (e[1] - m) * inv, (e[2] - m) * inv
        dd1 = a[0] * gc + g0 * (8.0 * d1 - 11.0 * d2)
        dd2 = a[1] * gc + g0 * (20.0 * d2 - 11.0 * d1) + g1 * (8.0 * d2 - 5.0 * d3)
        dd3 = a[2] * gc + g1 * (8.0 * d3 - 5.0 * d2) + g2 * (20.0 * d3 - 11.0 * d4)
        dd4 = a[3] * gc + g2 * (8.0 * d4 - 11.0 * d3)
        cells[0].append(-dd1)
        cells[1].append(dd1 - dd2)
        cells[2].append(dd2 - dd3 + gc)
        cells[3].append(dd3 - dd4)
        cells[4].append(dd4)
    return value, cells


def build_lines(scal, q, zlo, zhi, ylo, yhi, xin, uz, uy, ux):
    for c in range(5):
        uz[c, 0:30] = zlo[c, 0:30]
        uz[c, 30:120] = q[c, 0:OWN]
        uz[c, 120:150] = zhi[c, 0:30]
        uz[c, 150:160] = jnp.ones((10, LANES), jnp.float32)
        for z in range(CZ):
            uy[c, pl.ds(27 + z, CY, stride=CZ), :] = q[c, z * CY : (z + 1) * CY]
        flip = -1.0 if c == 2 else 1.0
        for g in range(3):
            low = scal[0] * flip * uy[c, (5 - g) * 9 : (6 - g) * 9] + scal[1] * uy[c, 27:36]
            uy[c, g * 9 : g * 9 + 9] = low + scal[2] * ylo[c, g * 9 : g * 9 + 9]
            high = scal[3] * flip * uy[c, (12 - g) * 9 : (13 - g) * 9] + scal[4] * uy[c, 108:117]
            uy[c, (13 + g) * 9 : (14 + g) * 9] = high + scal[5] * yhi[c, g * 9 : g * 9 + 9]
        uy[c, 144:160] = jnp.ones((16, LANES), jnp.float32)
        flip = -1.0 if c == 1 else 1.0
        own = q[c]
        partner = xin[c]
        value = own * lane_mask(ROWS, 3, 125)
        low = scal[8] * roll(partner, 6)
        high = scal[11] * roll(partner, 122)
        value = value + lane_mask(ROWS, 0, 3) * low + lane_mask(ROWS, 125, 128) * high
        for g in range(3):
            at_low = lane_mask(ROWS, g, g + 1)
            value = value + at_low * (
                scal[6] * flip * roll(own, -(5 - 2 * g)) + scal[7] * roll(own, g - 3)
            )
            at_high = lane_mask(ROWS, 125 + g, 126 + g)
            value = value + at_high * (
                scal[9] * flip * roll(own, 1 + 2 * g) + scal[10] * roll(own, 1 + g)
            )
        ux[c] = value


def cell_loop(name, u, plus, minus, smooth, rows):
    def body(i, carry):
        at = pl.ds(pl.multiple_of(i * 8, 8), 8)
        cells = [u[c, at, :] for c in range(5)]
        flux, sv = cell_terms(COMP[name], cells)
        for c in range(5):
            plus[c, at, :] = 0.5 * flux[c] + cells[c]
            minus[c, at, :] = 0.5 * flux[c] - cells[c]
        if smooth is not None:
            for c in range(4):
                smooth[c, at, :] = sv[c]
        return carry

    lax.fori_loop(0, rows // 8, body, 0)


def spread_rows(name, plus, minus, diffs, base):
    p = PITCH[name]
    at_plus, at_minus, count = FACE_ROWS[name]
    for c in range(5):
        for start, size in ((0, 56), (56, 48)):
            f = [plus[c, start + k * p : start + k * p + size] for k in range(5)]
            for i in range(4):
                diffs[i, c, at_plus + start : at_plus + start + size] = f[i + 1] - f[i]
            middle = f[2]
            f = [minus[c, start + k * p : start + k * p + size] for k in range(1, 6)]
            for i in range(4):
                diffs[i, c, at_minus + start : at_minus + start + size] = f[3 - i] - f[4 - i]
            if base is not None:
                base[c, at_plus // 2 + start : at_plus // 2 + start + size] = middle + f[2]


def spread_lanes(plus, minus, diffs, base):
    at_plus, at_minus, count = FACE_ROWS["x"]
    for c in range(5):
        for start in (0, 48):
            v = plus[c, start : start + 48]
            diff = roll(v, -1) - v
            for i in range(4):
                diffs[i, c, at_plus + start : at_plus + start + 48] = roll(diff, -i)
            m = minus[c, start : start + 48]
            diff = m - roll(m, -1)
            for i in range(4):
                diffs[i, c, at_minus + start : at_minus + start + 48] = roll(diff, i - 4)
            if base is not None:
                base[c, at_plus // 2 + start : at_plus // 2 + start + 48] = roll(v, -2) + roll(
                    m, -3
                )


def lap_rows(name, smooth, out):
    p = PITCH[name]
    out[0] = jnp.zeros((ROWS, LANES), jnp.float32)
    for c in range(4):
        coef = 0.02 if c < 3 else 0.03
        s = [smooth[c, k * p : k * p + OWN] for k in (2, 3, 4)]
        out[c + 1, 0:OWN] = coef * (s[2] - 2.0 * s[1] + s[0])


def gather_grad(prev, coef, scale, own, zlo, zhi, ylo, yhi, xin, total, grad):
    for c in range(5):
        x = lane_mask(ROWS, 122, 125) * roll(xin[c], 122) + lane_mask(ROWS, 3, 6) * roll(xin[c], 6)
        total[c] = coef * prev[c] + own[c] + x
        total[c, 0:30] = total[c, 0:30] + zlo[c, 0:30]
        total[c, 60:90] = total[c, 60:90] + zhi[c, 0:30]
        for z in range(CZ):
            low = z * CY
            total[c, low : low + 3] = total[c, low : low + 3] + ylo[c, pl.ds(z, 3, stride=CZ), :]
            total[c, low + 7 : low + 10] = (
                total[c, low + 7 : low + 10] + yhi[c, pl.ds(z, 3, stride=CZ), :]
            )
        if grad is not None:
            grad[c] = scale * total[c]


def grad_faces(grad, gz, gy, dface):
    for c in range(5):
        gz[c] = jnp.zeros((GPAD, LANES), jnp.float32)
        gy[c] = jnp.zeros((GPAD, LANES), jnp.float32)
        gz[c, 40 : 40 + OWN] = grad[c, 0:OWN]
        for z in range(CZ):
            gy[c, pl.ds(36 + z, CY, stride=CZ), :] = grad[c, z * CY : (z + 1) * CY]
        dz = gz[c, 40:144] - gz[c, 30:134]
        dy = gy[c, 36:140] - gy[c, 27:131]
        g = grad[c]
        dx = roll(g, -3) - roll(g, -2)
        dface[c, 0:104] = dz
        dface[c, 104:208] = dz
        dface[c, 208:312] = dy
        dface[c, 312:416] = dy
        dface[c, 416:512] = dx
        dface[c, 512:608] = dx


def pull_rows(name, dcell, plus, minus, gpad, u, out):
    p = PITCH[name]
    at_plus, at_minus, count = FACE_ROWS[name]
    for c in range(5):
        plus[c] = jnp.zeros((CELLS, LANES), jnp.float32)
        minus[c] = jnp.zeros((CELLS, LANES), jnp.float32)
        for k in range(5):
            low = k * p
            plus[c, low : low + 104] = (
                plus[c, low : low + 104] + dcell[k, c, at_plus : at_plus + 104]
            )
            low = (5 - k) * p
            minus[c, low : low + 104] = (
                minus[c, low : low + 104] + dcell[k, c, at_minus : at_minus + 104]
            )
        if c > 0:
            coef = 0.02 if c < 4 else 0.03
            g = [gpad[c, k * p : k * p + CELLS] for k in range(3)]
            out[c] = coef * (g[0] - 2.0 * g[1] + g[2])
    pull_cells(name, plus, minus, u, out, CELLS)


def pull_lanes(dcell, plus, minus, grad, u, out):
    at_plus, at_minus, count = FACE_ROWS["x"]
    for c in range(5):
        sp = dcell[0, c, at_plus : at_plus + ROWS]
        sm = roll(dcell[0, c, at_minus : at_minus + ROWS], 5)
        for k in range(1, 5):
            sp = sp + roll(dcell[k, c, at_plus : at_plus + ROWS], k)
            sm = sm + roll(dcell[k, c, at_minus : at_minus + ROWS], 5 - k)
        plus[c, 0:ROWS] = sp
        minus[c, 0:ROWS] = sm
        if c > 0:
            coef = 0.02 if c < 4 else 0.03
            g = grad[c]
            out[c, 0:ROWS] = coef * (roll(g, 1) - 2.0 * g + roll(g, -1))
    pull_cells("x", plus, minus, u, out, ROWS)


def pull_cells(name, plus, minus, u, out, rows):
    def body(i, carry):
        at = pl.ds(pl.multiple_of(i * 8, 8), 8)
        cells = [u[c, at, :] for c in range(5)]
        dp = [plus[c, at, :] for c in range(5)]
        dm = [minus[c, at, :] for c in range(5)]
        dsv = [out[c, at, :] for c in range(1, 5)]
        unused, back = jax.vjp(functools.partial(cell_terms, COMP[name]), cells)
        (du,) = back(([0.5 * (dp[c] + dm[c]) for c in range(5)], dsv))
        for c in range(5):
            out[c, at, :] = du[c] + dp[c] - dm[c]
        return carry

    lax.fori_loop(0, rows // 8, body, 0)


def section_kernel(mode, consts, *refs):
    refs = list(refs)
    take = lambda n: [refs.pop(0) for _ in range(n)]
    (scal,) = take(1)
    q, zlo, zhi, ylo, yhi, xin = take(6)
    if mode != "back":
        (first,) = take(1)
    if mode == "both":
        (prev,) = take(1)
    if mode == "back":
        prev, own_in, gzlo, gzhi, gylo, gyhi, gxin = take(7)
    if mode != "back":
        (state_out,) = take(1)
    if mode == "fwd":
        szlo, szhi, sylo, syhi = take(4)
    if mode == "back":
        (total,) = take(1)
    if mode != "fwd":
        own_out, dzlo, dzhi, dylo, dyhi, dx = take(6)
    uz, uy, ux, plus, minus, smooth, diffs = take(7)
    if mode != "back":
        base, tend_z, tend_y, tend_x, corr = take(5)
    else:
        base = None
    if mode != "fwd":
        grad, gz, gy, dface, dcell, dline, dline_y = take(7)

    build_lines(scal, q, zlo, zhi, ylo, yhi, xin, uz, uy, ux)
    wants = mode != "back"
    lap = smooth if wants else None
    for name, u, tend in (("z", uz, "tz"), ("y", uy, "ty")):
        cell_loop(name, u, plus, minus, lap, CELLS)
        spread_rows(name, plus, minus, diffs, base)
        if wants:
            lap_rows(name, smooth, tend_z if name == "z" else tend_y)
    cell_loop("x", ux, plus, minus, lap, ROWS)
    spread_lanes(plus, minus, diffs, base)
    if wants:
        tend_x[0] = jnp.zeros((ROWS, LANES), jnp.float32)
        for c in range(4):
            s = smooth[c, 0:ROWS]
            coef = 0.02 if c < 3 else 0.03
            tend_x[c + 1] = coef * (roll(s, 1) - 2.0 * s + roll(s, -1))

    if mode == "both":
        for c in range(5):
            grad[c] = consts["scale"] * prev[c]
    if mode == "back":
        gather_grad(
            prev, consts["coef"], consts["scale"], own_in, gzlo, gzhi, gylo, gyhi, gxin, total, grad
        )
    if mode != "fwd":
        grad_faces(grad, gz, gy, dface)

    def body(i, carry):
        at = pl.ds(pl.multiple_of(i * 8, 8), 8)
        d = [[diffs[k, c, at, :] for c in range(5)] for k in range(4)]
        g = None if mode == "fwd" else [dface[c, at, :] for c in range(5)]
        value, cells = weno_unit(d, scal, g, wants)
        if wants:
            for c in range(5):
                corr[c, at, :] = value[c]
        if cells is not None:
            for k in range(5):
                for c in range(5):
                    dcell[k, c, at, :] = cells[k][c]
        return carry

    lax.fori_loop(0, FACES // 8, body, 0)

    if wants:
        inside = lane_mask(OWN, 3, 125)
        for c in range(5):
            fz = base[c, 0:104] + corr[c, 0:104] + corr[c, 104:208]
            base[c, 0:104] = fz
            fy = base[c, 104:208] + corr[c, 208:312] + corr[c, 312:416]
            base[c, 104:208] = fy
            fx = base[c, 208:304] + corr[c, 416:512] + corr[c, 512:608]
            tend_z[c, 0:OWN] = tend_z[c, 0:OWN] + base[c, 0:OWN] - base[c, 10 : 10 + OWN]
            tend_y[c, 0:OWN] = tend_y[c, 0:OWN] + base[c, 104 : 104 + OWN] - base[c, 113 : 113 + OWN]
            tend_x[c] = tend_x[c] + roll(fx, 3) - roll(fx, 2)
            for z in range(CZ):
                low = z * CY
                tend_z[c, low : low + CY] = (
                    tend_z[c, low : low + CY] + tend_y[c, pl.ds(z, CY, stride=CZ), :]
                )
            t = (tend_z[c, 0:OWN] + tend_x[c, 0:OWN]) * (inside * DT)
            state_out[c, 0:OWN] = (
                consts["first"] * first[c, 0:OWN] + consts["last"] * (q[c, 0:OWN] + t)
            )
            state_out[c, OWN:ROWS] = jnp.ones((ROWS - OWN, LANES), jnp.float32)
            if mode == "fwd":
                szlo[c, 0:30] = state_out[c, 0:30]
                szhi[c, 0:30] = state_out[c, 60:90]
                for z in range(CZ):
                    low = z * CY
                    sylo[c, pl.ds(z, 3, stride=CZ), :] = state_out[c, low : low + 3]
                    syhi[c, pl.ds(z, 3, stride=CZ), :] = state_out[c, low + 7 : low + 10]

    if mode != "fwd":
        pull_rows("z", dcell, plus, minus, gz, uz, dline)
        for c in range(5):
            own_out[c, 0:OWN] = dline[c, 30:120]
            own_out[c, OWN:ROWS] = jnp.zeros((ROWS - OWN, LANES), jnp.float32)
            dzlo[c, 0:30] = dline[c, 0:30]
            dzhi[c, 0:30] = dline[c, 120:150]
        pull_rows("y", dcell, plus, minus, gy, uy, dline_y)
        for c in range(5):
            flip = -1.0 if c == 2 else 1.0
            dylo[c, 0:27] = dline_y[c, 0:27]
            dyhi[c, 0:27] = dline_y[c, 117:144]
            for g in range(3):
                low = dline_y[c, g * 9 : g * 9 + 9]
                high = dline_y[c, (13 + g) * 9 : (14 + g) * 9]
                at = (5 - g) * 9
                dline_y[c, at : at + 9] = dline_y[c, at : at + 9] + scal[0] * flip * low
                dline_y[c, 27:36] = dline_y[c, 27:36] + scal[1] * low
                at = (12 - g) * 9
                dline_y[c, at : at + 9] = dline_y[c, at : at + 9] + scal[3] * flip * high
                dline_y[c, 108:117] = dline_y[c, 108:117] + scal[4] * high
            for z in range(CZ):
                low = z * CY
                own_out[c, low : low + CY] = (
                    own_out[c, low : low + CY] + dline_y[c, pl.ds(27 + z, CY, stride=CZ), :]
                )
        pull_lanes(dcell, plus, minus, grad, ux, dline)
        rows_on = jnp.where(
            lax.broadcasted_iota(jnp.int32, (ROWS, LANES), 0) < OWN, 1.0, 0.0
        ).astype(jnp.float32)
        for c in range(5):
            flip = -1.0 if c == 1 else 1.0
            v = dline[c, 0:ROWS] * rows_on
            dx[c] = v * (
                lane_mask(ROWS, 0, 3) * scal[8] + lane_mask(ROWS, 125, 128) * scal[11]
            )
            acc = v + own_out[c]
            for g in range(3):
                low = v * lane_mask(ROWS, g, g + 1)
                high = v * lane_mask(ROWS, 125 + g, 126 + g)
                acc = acc + scal[6] * flip * roll(low, 5 - 2 * g) + scal[7] * roll(low, 3 - g)
                acc = acc + scal[9] * flip * roll(high, -1 - 2 * g) + scal[10] * roll(high, -1 - g)
            own_out[c] = acc * lane_mask(ROWS, 3, 125)


def finish_kernel(coef, prev, own, zlo, zhi, ylo, yhi, xin, total):
    gather_grad(prev, coef, None, own, zlo, zhi, ylo, yhi, xin, total, None)


FULL = (5, ROWS, LANES)
EDGE = (5, 32, LANES)


def shape(dims):
    return jax.ShapeDtypeStruct(dims, jnp.float32)


def vmem(dims):
    return pltpu.VMEM(dims, jnp.float32)


def section(mode, consts, *args):
    outs = []
    if mode != "back":
        outs.append(FULL)
    if mode == "fwd":
        outs += [EDGE] * 4
    if mode == "back":
        outs.append(FULL)
    if mode != "fwd":
        outs += [FULL] + [EDGE] * 4 + [FULL]
    line = (5, CELLS, LANES)
    scratch = [line, line, FULL, line, line, (4, CELLS, LANES), (4, 5, FACES, LANES)]
    if mode != "back":
        scratch += [(5, 304, LANES), FULL, FULL, FULL, (5, FACES, LANES)]
    if mode != "fwd":
        gpad = (5, GPAD, LANES)
        scratch += [FULL, gpad, gpad, (5, FACES, LANES), (5, 5, FACES, LANES), line, line]
    return pl.pallas_call(
        functools.partial(section_kernel, mode, consts),
        out_shape=[shape(s) for s in outs],
        in_specs=[pl.BlockSpec(memory_space=pltpu.SMEM)]
        + [pl.BlockSpec(memory_space=pltpu.VMEM)] * (len(args) - 1),
        out_specs=[pl.BlockSpec(memory_space=pltpu.VMEM)] * len(outs),
        scratch_shapes=[vmem(s) for s in scratch],
        compiler_params=pltpu.CompilerParams(vmem_limit_bytes=48 * 1024 * 1024),
        name="section_" + mode,
    )(*args)


def flat(field, fill):
    lanes = jnp.pad(
        field, ((0, 0), (0, 0), (0, 0), (3, 3)), constant_values=fill
    ).reshape(5, OWN, LANES)
    return jnp.pad(lanes, ((0, 0), (0, ROWS - OWN), (0, 0)), constant_values=fill)


def unflat(field):
    return field[:, :OWN].reshape(5, CZ, CY, LANES)[..., 3 : 3 + CX]


def swap(down, up, axis, periodic):
    count = lax.axis_size(axis)
    forward = [(i, i + 1) for i in range(count - 1)]
    if periodic:
        forward.append((count - 1, 0))
    backward = [(t, s) for s, t in forward]
    return lax.ppermute(up, axis, forward), lax.ppermute(down, axis, backward)


def exchange(full, zlo, zhi, ylo, yhi):
    from_z = swap(zlo, zhi, "gz", True)
    from_y = swap(ylo, yhi, "gy", False)
    partner = lax.ppermute(full, "gx", [(0, 1), (1, 0)])
    return (*from_z, *from_y, partner)


def on_device(density, momentum, energy, cotangent, bc_codes, weight_in, weight_out):
    state = flat(jnp.concatenate([density[None], momentum, energy[None]], 0), 1.0)
    cot = flat(cotangent, 0.0)
    y_place = lax.axis_index("gy")
    x_place = lax.axis_index("gx")
    edges = jnp.stack(
        [
            y_place == 0,
            y_place == lax.axis_size("gy") - 1,
            x_place == 0,
            x_place == lax.axis_size("gx") - 1,
        ]
    ).astype(jnp.float32)
    wall = (bc_codes == 0).astype(jnp.float32)
    sides = jnp.stack([edges * wall, edges * (1.0 - wall), 1.0 - edges], 1).reshape(12)
    scal = jnp.concatenate([sides, weight_in.reshape(-1), weight_out.reshape(-1)])

    rows = state[:, :OWN].reshape(5, CZ, CY, LANES)
    tail = lambda v, n: jnp.pad(v.reshape(5, n, LANES), ((0, 0), (0, 32 - n), (0, 0)))
    by_y = jnp.swapaxes(rows, 1, 2)
    halo_one = exchange(
        state,
        tail(rows[:, 0:3], 30),
        tail(rows[:, -3:], 30),
        tail(by_y[:, 0:3], 27),
        tail(by_y[:, -3:], 27),
    )
    one, *edge = section("fwd", dict(first=0.0, last=1.0), scal, state, *halo_one, state)
    halo_two = exchange(one, *edge)
    two, *edge = section("fwd", dict(first=0.75, last=0.25), scal, one, *halo_two, state)
    halo_three = exchange(two, *edge)
    new_state, own, *edge, dx = section(
        "both",
        dict(first=1.0 / 3.0, last=2.0 / 3.0, scale=DT * 2.0 / 3.0),
        scal,
        two,
        *halo_three,
        state,
        cot,
    )
    back = exchange(dx, *edge)
    grad_two, own, *edge, dx = section(
        "back", dict(coef=2.0 / 3.0, scale=0.25 * DT), scal, one, *halo_two, cot, own, *back
    )
    back = exchange(dx, *edge)
    grad_one, own, *edge, dx = section(
        "back", dict(coef=0.25, scale=DT), scal, state, *halo_one, grad_two, own, *back
    )
    back = exchange(dx, *edge)
    total = pl.pallas_call(
        functools.partial(finish_kernel, 1.0),
        out_shape=shape(FULL),
        name="finish",
    )(grad_one, own, *back)
    total = total + 0.75 * grad_two + (1.0 / 3.0) * cot
    return (unflat(new_state), unflat(total))


def solution(mesh):
    in_specs = (
        P(("groups", "gz"), "gy", "gx"),
        P(None, ("groups", "gz"), "gy", "gx"),
        P(("groups", "gz"), "gy", "gx"),
        P(None, ("groups", "gz"), "gy", "gx"),
        P("groups"),
        P(),
        P(),
    )
    out_specs = (P(None, ("groups", "gz"), "gy", "gx"), P(None, ("groups", "gz"), "gy", "gx"))
    return jax.shard_map(
        on_device, mesh=mesh, in_specs=in_specs, out_specs=out_specs, check_vma=False
    )
```

profile of v0, /device:TPU:0, one launch (start us, length us, event | category | flops | bytes accessed | tf_op | source)
XLA Modules:
  0.0 177.7 jit_solution(8635699045126204922)
XLA Ops:
  0.6 1.0 copy.19
  1.6 0.9 copy.20
  2.6 0.4 fusion.7
  3.0 0.5 collective-permute-start.4
  3.6 2.6 %collective-permute-start = (f32[5,32,128]{2,1,0:T(8,128)S(1)}, f32[5,32,128]{2,1,0:T(8,128)S(1)}, u32[]{:S(2)}, u32[]{:S(2)}) collective-permute-start(f32[5,32,128]{2,1,0:T(8,128)S(1)} %pad.30), channel_id=1, source_target_pairs={{0,4},{4,8},{8,12},{12,0},{1,5},{5,9},{9,13},{13,1},{2,6},{6,10},{... | collective-permute-start | bytes 245768 | tf_op jit(solution)/shard_map/ppermute | solution.py:516
  6.3 2.1 %collective-permute-start.1 = (f32[5,32,128]{2,1,0:T(8,128)S(1)}, f32[5,32,128]{2,1,0:T(8,128)S(1)}, u32[]{:S(2)}, u32[]{:S(2)}) collective-permute-start(f32[5,32,128]{2,1,0:T(8,128)S(1)} %pad.31), channel_id=1, source_target_pairs={{4,0},{8,4},{12,8},{0,12},{5,1},{9,5},{13,9},{1,13},{6,2},{10,6},{... | collective-permute-start | bytes 245768 | tf_op jit(solution)/shard_map/ppermute | solution.py:516
  8.4 3.6 %collective-permute-start.2 = (f32[5,32,128]{2,1,0:T(8,128)S(1)}, f32[5,32,128]{2,1,0:T(8,128)S(1)}, u32[]{:S(2)}, u32[]{:S(2)}) collective-permute-start(f32[5,32,128]{2,1,0:T(8,128)S(1)} %pad.32), channel_id=1, source_target_pairs={{0,2},{1,3},{4,6},{5,7},{8,10},{9,11},{12,14},{13,15},{16,18},{17,... | collective-permute-start | bytes 245768 | tf_op jit(solution)/shard_map/ppermute | solution.py:516
  12.1 1.3 collective-permute-start.3
  13.4 0.6 copy-done.11
  14.1 0.1 fusion.2
  14.2 0.1 fusion.6
  14.3 0.1 copy.17
  14.4 0.1 reshape.101
  14.4 0.6 copy-done.9
  15.0 0.1 copy.18
  15.1 0.1 reshape.103
  15.2 0.6 copy-done.10
  15.8 0.1 reshape.102
  15.9 0.1 pad_maximum_fusion.1.refs_0_
  16.0 2.5 %collective-permute-done.3.refs_5_ = f32[5,32,128]{2,1,0:T(8,128)S(1)} collective-permute-done((f32[5,32,128]{2,1,0:T(8,128)S(1)}, f32[5,32,128]{2,1,0:T(8,128)S(1)}, u32[]{:S(2)}, u32[]{:S(2)}) %collective-permute-start.3) | collective-permute-done | bytes 81952 | tf_op jit(solution)/shard_map/ppermute | solution.py:516
  18.5 13.0 %section_fwd.2 = (f32[5,96,128]{2,1,0:T(8,128)S(1)}, f32[5,32,128]{2,1,0:T(8,128)S(1)}, f32[5,32,128]{2,1,0:T(8,128)S(1)}, f32[5,32,128]{2,1,0:T(8,128)S(1)}, f32[5,32,128]{2,1,0:T(8,128)S(1)}) custom-call(f32[108]{0:T(128)S(1)} %pad_maximum_fusion.1.refs_0_, f32[5,96,128]{2,1,0:T(8,128)S(1)} %pad.29.refs_1_.refs_7_, ...), custom_call_target="tpu_custom_call" | custom-call | tf_op jit(solution)/shard_map/section_fwd/pallas_call | solution.py:487
  31.5 0.1 collective-permute-start.9
  31.6 3.8 %collective-permute-start.6 = (f32[5,32,128]{2,1,0:T(8,128)S(1)}, f32[5,32,128]{2,1,0:T(8,128)S(1)}, u32[]{:S(2)}, u32[]{:S(2)}) collective-permute-start(f32[5,32,128]{2,1,0:T(8,128)S(1)} %get-tuple-element.35), channel_id=1, source_target_pairs={{4,0},{8,4},{12,8},{0,12},{5,1},{9,5},{13,9},{1,13},{6,2},{10,6},{... | collective-permute-start | bytes 245768 | tf_op jit(solution)/shard_map/ppermute | solution.py:516
  35.4 2.1 %collective-permute-start.7 = (f32[5,32,128]{2,1,0:T(8,128)S(1)}, f32[5,32,128]{2,1,0:T(8,128)S(1)}, u32[]{:S(2)}, u32[]{:S(2)}) collective-permute-start(f32[5,32,128]{2,1,0:T(8,128)S(1)} %get-tuple-element.36), channel_id=1, source_target_pairs={{0,2},{1,3},{4,6},{5,7},{8,10},{9,11},{12,14},{13,15},{16,18},{17,... | collective-permute-start | bytes 245768 | tf_op jit(solution)/shard_map/ppermute | solution.py:516
  37.5 1.4 collective-permute-start.8
  39.0 0.6 collective-permute-done.7.refs_4_
  39.6 4.4 %collective-permute-done.8.refs_5_ = f32[5,32,128]{2,1,0:T(8,128)S(1)} collective-permute-done((f32[5,32,128]{2,1,0:T(8,128)S(1)}, f32[5,32,128]{2,1,0:T(8,128)S(1)}, u32[]{:S(2)}, u32[]{:S(2)}) %collective-permute-start.8) | collective-permute-done | bytes 81952 | tf_op jit(solution)/shard_map/ppermute | solution.py:516
  44.0 13.0 %section_fwd.3 = (f32[5,96,128]{2,1,0:T(8,128)S(1)}, f32[5,32,128]{2,1,0:T(8,128)S(1)}, f32[5,32,128]{2,1,0:T(8,128)S(1)}, f32[5,32,128]{2,1,0:T(8,128)S(1)}, f32[5,32,128]{2,1,0:T(8,128)S(1)}) custom-call(f32[108]{0:T(128)S(1)} %pad_maximum_fusion.1.refs_0_, f32[5,96,128]{2,1,0:T(8,128)S(1)} %get-tuple-element.33.refs_1_, ...), custom_call_target="tpu_custom_call" | custom-call | tf_op jit(solution)/shard_map/section_fwd/pallas_call | solution.py:487
  57.0 0.1 collective-permute-start.14
  57.2 3.8 %collective-permute-start.11 = (f32[5,32,128]{2,1,0:T(8,128)S(1)}, f32[5,32,128]{2,1,0:T(8,128)S(1)}, u32[]{:S(2)}, u32[]{:S(2)}) collective-permute-start(f32[5,32,128]{2,1,0:T(8,128)S(1)} %get-tuple-element.40), channel_id=1, source_target_pairs={{4,0},{8,4},{12,8},{0,12},{5,1},{9,5},{13,9},{1,13},{6,2},{10,6},{... | collective-permute-start | bytes 245768 | tf_op jit(solution)/shard_map/ppermute | solution.py:516
  61.0 1.5 collective-permute-start.12
  62.5 1.3 collective-permute-start.13
  63.8 0.2 pad.34
  64.1 0.1 collective-permute-done.10.refs_2_
  64.2 0.4 collective-permute-done.12.refs_4_
  64.6 4.3 %collective-permute-done.13.refs_5_ = f32[5,32,128]{2,1,0:T(8,128)S(1)} collective-permute-done((f32[5,32,128]{2,1,0:T(8,128)S(1)}, f32[5,32,128]{2,1,0:T(8,128)S(1)}, u32[]{:S(2)}, u32[]{:S(2)}) %collective-permute-start.13) | collective-permute-done | bytes 81952 | tf_op jit(solution)/shard_map/ppermute | solution.py:516
  68.9 23.5 %section_both.1 = (f32[5,96,128]{2,1,0:T(8,128)S(1)}, f32[5,96,128]{2,1,0:T(8,128)S(1)}, f32[5,32,128]{2,1,0:T(8,128)S(1)}, f32[5,32,128]{2,1,0:T(8,128)S(1)}, f...) custom-call(f32[108]{0:T(128)S(1)} %pad_maximum_fusion.1.refs_0_, ...), custom_call_target="tpu_custom_call" | custom-call | tf_op jit(solution)/shard_map/section_both/pallas_call | solution.py:487
  92.4 0.1 collective-permute-start.19
  92.6 3.8 %collective-permute-start.16 = (f32[5,32,128]{2,1,0:T(8,128)S(1)}, f32[5,32,128]{2,1,0:T(8,128)S(1)}, u32[]{:S(2)}, u32[]{:S(2)}) collective-permute-start(f32[5,32,128]{2,1,0:T(8,128)S(1)} %get-tuple-element.46), channel_id=1, source_target_pairs={{4,0},{8,4},{12,8},{0,12},{5,1},{9,5},{13,9},{1,13},{6,2},{10,6},{... | collective-permute-start | bytes 245768 | tf_op jit(solution)/shard_map/ppermute | solution.py:516
  96.4 1.5 collective-permute-start.17
  97.9 1.5 collective-permute-start.18
  99.4 0.2 collective-permute-done.15.refs_9_
  99.6 0.4 collective-permute-done.17.refs_11_
  100.0 4.5 %collective-permute-done.18.refs_12_ = f32[5,32,128]{2,1,0:T(8,128)S(1)} collective-permute-done((f32[5,32,128]{2,1,0:T(8,128)S(1)}, f32[5,32,128]{2,1,0:T(8,128)S(1)}, u32[]{:S(2)}, u32[]{:S(2)}) %collective-permute-start.18) | collective-permute-done | bytes 81952 | tf_op jit(solution)/shard_map/ppermute | solution.py:516
  104.4 21.7 %section_back.2 = (f32[5,96,128]{2,1,0:T(8,128)S(1)}, f32[5,96,128]{2,1,0:T(8,128)S(1)}, f32[5,32,128]{2,1,0:T(8,128)S(1)}, f32[5,32,128]{2,1,0:T(8,128)S(1)}, f...) custom-call(f32[108]{0:T(128)S(1)} %pad_maximum_fusion.1.refs_0_, ...), custom_call_target="tpu_custom_call" | custom-call | tf_op jit(solution)/shard_map/section_back/pallas_call | solution.py:487
  126.3 3.8 %collective-permute-start.21 = (f32[5,32,128]{2,1,0:T(8,128)S(1)}, f32[5,32,128]{2,1,0:T(8,128)S(1)}, u32[]{:S(2)}, u32[]{:S(2)}) collective-permute-start(f32[5,32,128]{2,1,0:T(8,128)S(1)} %get-tuple-element.53), channel_id=1, source_target_pairs={{4,0},{8,4},{12,8},{0,12},{5,1},{9,5},{13,9},{1,13},{6,2},{10,6},{... | collective-permute-start | bytes 245768 | tf_op jit(solution)/shard_map/ppermute | solution.py:516
  130.1 1.5 collective-permute-start.22
  131.7 1.3 collective-permute-start.23
  133.0 0.4 collective-permute-done.20.refs_9_
  133.3 0.4 collective-permute-done.22.refs_11_
  133.7 4.3 %collective-permute-done.23.refs_12_ = f32[5,32,128]{2,1,0:T(8,128)S(1)} collective-permute-done((f32[5,32,128]{2,1,0:T(8,128)S(1)}, f32[5,32,128]{2,1,0:T(8,128)S(1)}, u32[]{:S(2)}, u32[]{:S(2)}) %collective-permute-start.23) | collective-permute-done | bytes 81952 | tf_op jit(solution)/shard_map/ppermute | solution.py:516
  138.0 21.7 %section_back.3 = (f32[5,96,128]{2,1,0:T(8,128)S(1)}, f32[5,96,128]{2,1,0:T(8,128)S(1)}, f32[5,32,128]{2,1,0:T(8,128)S(1)}, f32[5,32,128]{2,1,0:T(8,128)S(1)}, f...) custom-call(f32[108]{0:T(128)S(1)} %pad_maximum_fusion.1.refs_0_, ...), custom_call_target="tpu_custom_call" | custom-call | tf_op jit(solution)/shard_map/section_back/pallas_call | solution.py:487
  159.7 0.7 copy-done
  160.4 0.7 copy-done.1
  161.1 3.8 %collective-permute-start.26 = (f32[5,32,128]{2,1,0:T(8,128)S(1)}, f32[5,32,128]{2,1,0:T(8,128)S(1)}, u32[]{:S(2)}, u32[]{:S(2)}) collective-permute-start(f32[5,32,128]{2,1,0:T(8,128)S(1)} %get-tuple-element.60), channel_id=1, source_target_pairs={{4,0},{8,4},{12,8},{0,12},{5,1},{9,5},{13,9},{1,13},{6,2},{10,6},{... | collective-permute-start | bytes 245768 | tf_op jit(solution)/shard_map/ppermute | solution.py:516
  164.9 1.5 collective-permute-start.27
  166.4 1.3 collective-permute-start.28
  167.8 0.9 slice.37
  168.7 4.1 %collective-permute-done.28.yhi = f32[5,32,128]{2,1,0:T(8,128)S(1)} collective-permute-done((f32[5,32,128]{2,1,0:T(8,128)S(1)}, f32[5,32,128]{2,1,0:T(8,128)S(1)}, u32[]{:S(2)}, u32[]{:S(2)}) %collective-permute-start.28) | collective-permute-done | bytes 81952 | tf_op jit(solution)/shard_map/ppermute | solution.py:516
  172.8 0.6 copy-done.8
  173.4 0.1 copy-done.3
  173.5 2.3 %finish.1 = f32[5,96,128]{2,1,0:T(8,128)} custom-call(f32[5,96,128]{2,1,0:T(8,128)} %copy-done, f32[5,96,128]{2,1,0:T(8,128)} %copy-done.1, f32[5,32,128]{2,1,0:T(8,128)} %copy-done.5, f32[5,32,128]{2,1,0:T(8,128)} %copy-done.6, f32[5,32,128]{2,1,0:T(8,128)} %copy-done.7, f32[5,32,128]{2,1,0:T(8,128)} %copy-done.8, f32[5,96,128]{2,1,0:T(8,128)} %copy-done.3), custom_call_target="tpu_custom_call" | custom-call | tf_op jit(solution)/shard_map/finish/pallas_call | solution.py:575
  175.8 1.0 fusion.1
  176.8 0.9 slice.40
  (61 shorter events, 0.7 us)
Async XLA Ops:
  0.6 1.9 %copy-start.4 = (f32[3,9,10,122]{3,0,2,1:T(4,128)S(1)}, f32[3,9,10,122]{3,0,2,1:T(4,128)}, u32[]{:S(2)}) copy-start(f32[3,9,10,122]{3,0,2,1:T(4,128)} %param.8) | copy-start | bytes 395284
  3.0 15.4 %collective-permute-start.4 = (f32[5,96,128]{2,1,0:T(8,128)S(1)}, f32[5,96,128]{2,1,0:T(8,128)S(1)}, u32[]{:S(2)}, u32[]{:S(2)}) collective-permute-start(f32[5,96,128]{2,1,0:T(8,128)S(1)} %pad.29.refs_1_.refs_7_), channel_id=1, source_target_pairs={{0,1},{1,0},{2,3},{3,2},{4,5},{5,4},{6,7},{7,6},{8,9},{9,8},{10,11... | collective-permute-start | bytes 737288 | tf_op jit(solution)/shard_map/ppermute | solution.py:522
  3.6 12.4 %collective-permute-start = (f32[5,32,128]{2,1,0:T(8,128)S(1)}, f32[5,32,128]{2,1,0:T(8,128)S(1)}, u32[]{:S(2)}, u32[]{:S(2)}) collective-permute-start(f32[5,32,128]{2,1,0:T(8,128)S(1)} %pad.30), channel_id=1, source_target_pairs={{0,4},{4,8},{8,12},{12,0},{1,5},{5,9},{9,13},{13,1},{2,6},{6,10},{... | collective-permute-start | bytes 245768 | tf_op jit(solution)/shard_map/ppermute | solution.py:516
  6.3 9.7 %collective-permute-start.1 = (f32[5,32,128]{2,1,0:T(8,128)S(1)}, f32[5,32,128]{2,1,0:T(8,128)S(1)}, u32[]{:S(2)}, u32[]{:S(2)}) collective-permute-start(f32[5,32,128]{2,1,0:T(8,128)S(1)} %pad.31), channel_id=1, source_target_pairs={{4,0},{8,4},{12,8},{0,12},{5,1},{9,5},{13,9},{1,13},{6,2},{10,6},{... | collective-permute-start | bytes 245768 | tf_op jit(solution)/shard_map/ppermute | solution.py:516
  8.4 7.5 %collective-permute-start.2 = (f32[5,32,128]{2,1,0:T(8,128)S(1)}, f32[5,32,128]{2,1,0:T(8,128)S(1)}, u32[]{:S(2)}, u32[]{:S(2)}) collective-permute-start(f32[5,32,128]{2,1,0:T(8,128)S(1)} %pad.32), channel_id=1, source_target_pairs={{0,2},{1,3},{4,6},{5,7},{8,10},{9,11},{12,14},{13,15},{16,18},{17,... | collective-permute-start | bytes 245768 | tf_op jit(solution)/shard_map/ppermute | solution.py:516
  12.1 6.3 %collective-permute-start.3 = (f32[5,32,128]{2,1,0:T(8,128)S(1)}, f32[5,32,128]{2,1,0:T(8,128)S(1)}, u32[]{:S(2)}, u32[]{:S(2)}) collective-permute-start(f32[5,32,128]{2,1,0:T(8,128)S(1)} %pad.33), channel_id=1, source_target_pairs={{2,0},{3,1},{6,4},{7,5},{10,8},{11,9},{14,12},{15,13},{18,16},{19,... | collective-permute-start | bytes 245768 | tf_op jit(solution)/shard_map/ppermute | solution.py:516
  13.4 0.7 copy-start.11
  14.4 0.7 copy-start.9
  15.1 0.7 copy-start.10
  31.5 12.5 %collective-permute-start.9 = (f32[5,96,128]{2,1,0:T(8,128)S(1)}, f32[5,96,128]{2,1,0:T(8,128)S(1)}, u32[]{:S(2)}, u32[]{:S(2)}) collective-permute-start(f32[5,96,128]{2,1,0:T(8,128)S(1)} %get-tuple-element.33.refs_1_), channel_id=1, source_target_pairs={{0,1},{1,0},{2,3},{3,2},{4,5},{5,4},{6,7},{7,6},{8,9},{9,8},{10,11... | collective-permute-start | bytes 737288 | tf_op jit(solution)/shard_map/ppermute | solution.py:522
  31.5 7.4 %collective-permute-start.5 = (f32[5,32,128]{2,1,0:T(8,128)S(1)}, f32[5,32,128]{2,1,0:T(8,128)S(1)}, u32[]{:S(2)}, u32[]{:S(2)}) collective-permute-start(f32[5,32,128]{2,1,0:T(8,128)S(1)} %get-tuple-element.34), channel_id=1, source_target_pairs={{0,4},{4,8},{8,12},{12,0},{1,5},{5,9},{9,13},{13,1},{2,6},{6,10},{... | collective-permute-start | bytes 245768 | tf_op jit(solution)/shard_map/ppermute | solution.py:516
  31.6 7.4 %collective-permute-start.6 = (f32[5,32,128]{2,1,0:T(8,128)S(1)}, f32[5,32,128]{2,1,0:T(8,128)S(1)}, u32[]{:S(2)}, u32[]{:S(2)}) collective-permute-start(f32[5,32,128]{2,1,0:T(8,128)S(1)} %get-tuple-element.35), channel_id=1, source_target_pairs={{4,0},{8,4},{12,8},{0,12},{5,1},{9,5},{13,9},{1,13},{6,2},{10,6},{... | collective-permute-start | bytes 245768 | tf_op jit(solution)/shard_map/ppermute | solution.py:516
  35.4 4.1 %collective-permute-start.7 = (f32[5,32,128]{2,1,0:T(8,128)S(1)}, f32[5,32,128]{2,1,0:T(8,128)S(1)}, u32[]{:S(2)}, u32[]{:S(2)}) collective-permute-start(f32[5,32,128]{2,1,0:T(8,128)S(1)} %get-tuple-element.36), channel_id=1, source_target_pairs={{0,2},{1,3},{4,6},{5,7},{8,10},{9,11},{12,14},{13,15},{16,18},{17,... | collective-permute-start | bytes 245768 | tf_op jit(solution)/shard_map/ppermute | solution.py:516
  37.5 26.3 %copy-start.2 = (f32[5,9,10,122]{3,2,1,0:T(8,128)S(1)}, f32[5,9,10,122]{3,2,1,0:T(8,128)}, u32[]{:S(2)}) copy-start(f32[5,9,10,122]{3,2,1,0:T(8,128)} %param.10) | copy-start | bytes 658804
  37.5 6.5 %collective-permute-start.8 = (f32[5,32,128]{2,1,0:T(8,128)S(1)}, f32[5,32,128]{2,1,0:T(8,128)S(1)}, u32[]{:S(2)}, u32[]{:S(2)}) collective-permute-start(f32[5,32,128]{2,1,0:T(8,128)S(1)} %get-tuple-element.37), channel_id=1, source_target_pairs={{2,0},{3,1},{6,4},{7,5},{10,8},{11,9},{14,12},{15,13},{18,16},{19,... | collective-permute-start | bytes 245768 | tf_op jit(solution)/shard_map/ppermute | solution.py:516
  57.0 11.8 %collective-permute-start.14 = (f32[5,96,128]{2,1,0:T(8,128)S(1)}, f32[5,96,128]{2,1,0:T(8,128)S(1)}, u32[]{:S(2)}, u32[]{:S(2)}) collective-permute-start(f32[5,96,128]{2,1,0:T(8,128)S(1)} %get-tuple-element.38.refs_1_), channel_id=1, source_target_pairs={{0,1},{1,0},{2,3},{3,2},{4,5},{5,4},{6,7},{7,6},{8,9},{9,8},{10,11... | collective-permute-start | bytes 737288 | tf_op jit(solution)/shard_map/ppermute | solution.py:522
  57.1 7.1 %collective-permute-start.10 = (f32[5,32,128]{2,1,0:T(8,128)S(1)}, f32[5,32,128]{2,1,0:T(8,128)S(1)}, u32[]{:S(2)}, u32[]{:S(2)}) collective-permute-start(f32[5,32,128]{2,1,0:T(8,128)S(1)} %get-tuple-element.39), channel_id=1, source_target_pairs={{0,4},{4,8},{8,12},{12,0},{1,5},{5,9},{9,13},{13,1},{2,6},{6,10},{... | collective-permute-start | bytes 245768 | tf_op jit(solution)/shard_map/ppermute | solution.py:516
  57.2 7.0 %collective-permute-start.11 = (f32[5,32,128]{2,1,0:T(8,128)S(1)}, f32[5,32,128]{2,1,0:T(8,128)S(1)}, u32[]{:S(2)}, u32[]{:S(2)}) collective-permute-start(f32[5,32,128]{2,1,0:T(8,128)S(1)} %get-tuple-element.40), channel_id=1, source_target_pairs={{4,0},{8,4},{12,8},{0,12},{5,1},{9,5},{13,9},{1,13},{6,2},{10,6},{... | collective-permute-start | bytes 245768 | tf_op jit(solution)/shard_map/ppermute | solution.py:516
  61.0 3.6 %collective-permute-start.12 = (f32[5,32,128]{2,1,0:T(8,128)S(1)}, f32[5,32,128]{2,1,0:T(8,128)S(1)}, u32[]{:S(2)}, u32[]{:S(2)}) collective-permute-start(f32[5,32,128]{2,1,0:T(8,128)S(1)} %get-tuple-element.41), channel_id=1, source_target_pairs={{0,2},{1,3},{4,6},{5,7},{8,10},{9,11},{12,14},{13,15},{16,18},{17,... | collective-permute-start | bytes 245768 | tf_op jit(solution)/shard_map/ppermute | solution.py:516
  62.5 6.3 %collective-permute-start.13 = (f32[5,32,128]{2,1,0:T(8,128)S(1)}, f32[5,32,128]{2,1,0:T(8,128)S(1)}, u32[]{:S(2)}, u32[]{:S(2)}) collective-permute-start(f32[5,32,128]{2,1,0:T(8,128)S(1)} %get-tuple-element.42), channel_id=1, source_target_pairs={{2,0},{3,1},{6,4},{7,5},{10,8},{11,9},{14,12},{15,13},{18,16},{19,... | collective-permute-start | bytes 245768 | tf_op jit(solution)/shard_map/ppermute | solution.py:516
  92.4 12.0 %collective-permute-start.19 = (f32[5,96,128]{2,1,0:T(8,128)S(1)}, f32[5,96,128]{2,1,0:T(8,128)S(1)}, u32[]{:S(2)}, u32[]{:S(2)}) collective-permute-start(f32[5,96,128]{2,1,0:T(8,128)S(1)} %get-tuple-element.49), channel_id=1, source_target_pairs={{0,1},{1,0},{2,3},{3,2},{4,5},{5,4},{6,7},{7,6},{8,9},{9,8},{10,11... | collective-permute-start | bytes 737288 | tf_op jit(solution)/shard_map/ppermute | solution.py:522
  92.5 7.1 %collective-permute-start.15 = (f32[5,32,128]{2,1,0:T(8,128)S(1)}, f32[5,32,128]{2,1,0:T(8,128)S(1)}, u32[]{:S(2)}, u32[]{:S(2)}) collective-permute-start(f32[5,32,128]{2,1,0:T(8,128)S(1)} %get-tuple-element.45), channel_id=1, source_target_pairs={{0,4},{4,8},{8,12},{12,0},{1,5},{5,9},{9,13},{13,1},{2,6},{6,10},{... | collective-permute-start | bytes 245768 | tf_op jit(solution)/shard_map/ppermute | solution.py:516
  92.6 7.0 %collective-permute-start.16 = (f32[5,32,128]{2,1,0:T(8,128)S(1)}, f32[5,32,128]{2,1,0:T(8,128)S(1)}, u32[]{:S(2)}, u32[]{:S(2)}) collective-permute-start(f32[5,32,128]{2,1,0:T(8,128)S(1)} %get-tuple-element.46), channel_id=1, source_target_pairs={{4,0},{8,4},{12,8},{0,12},{5,1},{9,5},{13,9},{1,13},{6,2},{10,6},{... | collective-permute-start | bytes 245768 | tf_op jit(solution)/shard_map/ppermute | solution.py:516
  96.4 3.6 %collective-permute-start.17 = (f32[5,32,128]{2,1,0:T(8,128)S(1)}, f32[5,32,128]{2,1,0:T(8,128)S(1)}, u32[]{:S(2)}, u32[]{:S(2)}) collective-permute-start(f32[5,32,128]{2,1,0:T(8,128)S(1)} %get-tuple-element.47), channel_id=1, source_target_pairs={{0,2},{1,3},{4,6},{5,7},{8,10},{9,11},{12,14},{13,15},{16,18},{17,... | collective-permute-start | bytes 245768 | tf_op jit(solution)/shard_map/ppermute | solution.py:516
  97.9 6.5 %collective-permute-start.18 = (f32[5,32,128]{2,1,0:T(8,128)S(1)}, f32[5,32,128]{2,1,0:T(8,128)S(1)}, u32[]{:S(2)}, u32[]{:S(2)}) collective-permute-start(f32[5,32,128]{2,1,0:T(8,128)S(1)} %get-tuple-element.48), channel_id=1, source_target_pairs={{2,0},{3,1},{6,4},{7,5},{10,8},{11,9},{14,12},{15,13},{18,16},{19,... | collective-permute-start | bytes 245768 | tf_op jit(solution)/shard_map/ppermute | solution.py:516
  126.1 11.8 %collective-permute-start.24 = (f32[5,96,128]{2,1,0:T(8,128)S(1)}, f32[5,96,128]{2,1,0:T(8,128)S(1)}, u32[]{:S(2)}, u32[]{:S(2)}) collective-permute-start(f32[5,96,128]{2,1,0:T(8,128)S(1)} %get-tuple-element.56), channel_id=1, source_target_pairs={{0,1},{1,0},{2,3},{3,2},{4,5},{5,4},{6,7},{7,6},{8,9},{9,8},{10,11... | collective-permute-start | bytes 737288 | tf_op jit(solution)/shard_map/ppermute | solution.py:522
  126.2 7.1 %collective-permute-start.20 = (f32[5,32,128]{2,1,0:T(8,128)S(1)}, f32[5,32,128]{2,1,0:T(8,128)S(1)}, u32[]{:S(2)}, u32[]{:S(2)}) collective-permute-start(f32[5,32,128]{2,1,0:T(8,128)S(1)} %get-tuple-element.52), channel_id=1, source_target_pairs={{0,4},{4,8},{8,12},{12,0},{1,5},{5,9},{9,13},{13,1},{2,6},{6,10},{... | collective-permute-start | bytes 245768 | tf_op jit(solution)/shard_map/ppermute | solution.py:516
  126.3 7.0 %collective-permute-start.21 = (f32[5,32,128]{2,1,0:T(8,128)S(1)}, f32[5,32,128]{2,1,0:T(8,128)S(1)}, u32[]{:S(2)}, u32[]{:S(2)}) collective-permute-start(f32[5,32,128]{2,1,0:T(8,128)S(1)} %get-tuple-element.53), channel_id=1, source_target_pairs={{4,0},{8,4},{12,8},{0,12},{5,1},{9,5},{13,9},{1,13},{6,2},{10,6},{... | collective-permute-start | bytes 245768 | tf_op jit(solution)/shard_map/ppermute | solution.py:516
  130.1 3.6 %collective-permute-start.22 = (f32[5,32,128]{2,1,0:T(8,128)S(1)}, f32[5,32,128]{2,1,0:T(8,128)S(1)}, u32[]{:S(2)}, u32[]{:S(2)}) collective-permute-start(f32[5,32,128]{2,1,0:T(8,128)S(1)} %get-tuple-element.54), channel_id=1, source_target_pairs={{0,2},{1,3},{4,6},{5,7},{8,10},{9,11},{12,14},{13,15},{16,18},{17,... | collective-permute-start | bytes 245768 | tf_op jit(solution)/shard_map/ppermute | solution.py:516
  131.7 6.3 %collective-permute-start.23 = (f32[5,32,128]{2,1,0:T(8,128)S(1)}, f32[5,32,128]{2,1,0:T(8,128)S(1)}, u32[]{:S(2)}, u32[]{:S(2)}) collective-permute-start(f32[5,32,128]{2,1,0:T(8,128)S(1)} %get-tuple-element.55), channel_id=1, source_target_pairs={{2,0},{3,1},{6,4},{7,5},{10,8},{11,9},{14,12},{15,13},{18,16},{19,... | collective-permute-start | bytes 245768 | tf_op jit(solution)/shard_map/ppermute | solution.py:516
  159.7 0.7 copy-start
  160.4 0.7 copy-start.1
  161.1 11.7 %collective-permute-start.29 = (f32[5,96,128]{2,1,0:T(8,128)S(1)}, f32[5,96,128]{2,1,0:T(8,128)S(1)}, u32[]{:S(2)}, u32[]{:S(2)}) collective-permute-start(f32[5,96,128]{2,1,0:T(8,128)S(1)} %get-tuple-element.63), channel_id=1, source_target_pairs={{0,1},{1,0},{2,3},{3,2},{4,5},{5,4},{6,7},{7,6},{8,9},{9,8},{10,11... | collective-permute-start | bytes 737288 | tf_op jit(solution)/shard_map/ppermute | solution.py:522
  161.1 7.6 %collective-permute-start.25 = (f32[5,32,128]{2,1,0:T(8,128)S(1)}, f32[5,32,128]{2,1,0:T(8,128)S(1)}, u32[]{:S(2)}, u32[]{:S(2)}) collective-permute-start(f32[5,32,128]{2,1,0:T(8,128)S(1)} %get-tuple-element.59), channel_id=1, source_target_pairs={{0,4},{4,8},{8,12},{12,0},{1,5},{5,9},{9,13},{13,1},{2,6},{6,10},{... | collective-permute-start | bytes 245768 | tf_op jit(solution)/shard_map/ppermute | solution.py:516
  161.1 7.6 %collective-permute-start.26 = (f32[5,32,128]{2,1,0:T(8,128)S(1)}, f32[5,32,128]{2,1,0:T(8,128)S(1)}, u32[]{:S(2)}, u32[]{:S(2)}) collective-permute-start(f32[5,32,128]{2,1,0:T(8,128)S(1)} %get-tuple-element.60), channel_id=1, source_target_pairs={{4,0},{8,4},{12,8},{0,12},{5,1},{9,5},{13,9},{1,13},{6,2},{10,6},{... | collective-permute-start | bytes 245768 | tf_op jit(solution)/shard_map/ppermute | solution.py:516
  164.9 3.8 %collective-permute-start.27 = (f32[5,32,128]{2,1,0:T(8,128)S(1)}, f32[5,32,128]{2,1,0:T(8,128)S(1)}, u32[]{:S(2)}, u32[]{:S(2)}) collective-permute-start(f32[5,32,128]{2,1,0:T(8,128)S(1)} %get-tuple-element.61), channel_id=1, source_target_pairs={{0,2},{1,3},{4,6},{5,7},{8,10},{9,11},{12,14},{13,15},{16,18},{17,... | collective-permute-start | bytes 245768 | tf_op jit(solution)/shard_map/ppermute | solution.py:516
  166.4 6.3 %collective-permute-start.28 = (f32[5,32,128]{2,1,0:T(8,128)S(1)}, f32[5,32,128]{2,1,0:T(8,128)S(1)}, u32[]{:S(2)}, u32[]{:S(2)}) collective-permute-start(f32[5,32,128]{2,1,0:T(8,128)S(1)} %get-tuple-element.62), channel_id=1, source_target_pairs={{2,0},{3,1},{6,4},{7,5},{10,8},{11,9},{14,12},{15,13},{18,16},{19,... | collective-permute-start | bytes 245768 | tf_op jit(solution)/shard_map/ppermute | solution.py:516
  168.7 4.1 %copy-start.5 = (f32[5,32,128]{2,1,0:T(8,128)}, f32[5,32,128]{2,1,0:T(8,128)S(1)}, u32[]{:S(2)}) copy-start(f32[5,32,128]{2,1,0:T(8,128)S(1)} %collective-permute-done.25.zlo) | copy-start | bytes 245764
  168.7 4.1 %copy-start.6 = (f32[5,32,128]{2,1,0:T(8,128)}, f32[5,32,128]{2,1,0:T(8,128)S(1)}, u32[]{:S(2)}) copy-start(f32[5,32,128]{2,1,0:T(8,128)S(1)} %collective-permute-done.26.zhi) | copy-start | bytes 245764
  168.7 4.1 %copy-start.7 = (f32[5,32,128]{2,1,0:T(8,128)}, f32[5,32,128]{2,1,0:T(8,128)S(1)}, u32[]{:S(2)}) copy-start(f32[5,32,128]{2,1,0:T(8,128)S(1)} %collective-permute-done.27.ylo) | copy-start | bytes 245764
  172.8 0.6 copy-start.8
  172.8 0.7 copy-start.3
where the time goes:
time: 178 us
  Pallas kernels  95.2 us (53%)
  starting transfers between devices  44.8 us (25%)
  waiting for transfers between devices  26.4 us (15%)
  local copies, waits for them, and re-layouts  8.58 us (5%)
    pallas_call x5, Pallas kernels, section(): pl.pallas_call(functools.partial(section_kernel, mode, consts), out_shape...  92.9 us
    ppermute x24, starting transfers between devices, swap(): return (lax.ppermute(up, axis, forward), lax.ppermute(down, axis, backward))  44 us
    ppermute x24, waiting for transfers between devices, swap(): return (lax.ppermute(up, axis, forward), lax.ppermute(down, axis, backward))  26.4 us
    unnamed x25, local copies, waits for them, and re-layouts  4.05 us
  transfers between devices with their start and end apart: 30, of which 13 were waited for; matrix products, arithmetic and copies ran while one was open for 1% of the time, Pallas kernels for 0%

commit v1 on v0

--- a/solution.py
+++ b/solution.py
@@ -307,32 +307,15 @@
     lax.fori_loop(0, rows // 8, body, 0)
 
 
-def section_kernel(mode, consts, *refs):
-    refs = list(refs)
-    take = lambda n: [refs.pop(0) for _ in range(n)]
-    (scal,) = take(1)
-    q, zlo, zhi, ylo, yhi, xin = take(6)
-    if mode != "back":
-        (first,) = take(1)
-    if mode == "both":
-        (prev,) = take(1)
+def section(mode, consts, scal, q, halo, first, prev, own_in, halo_grad, state_out, sends, total,
+            own_out, grad_sends, dx, work):
+    zlo, zhi, ylo, yhi, xin = halo
+    uz, uy, ux, plus, minus, smooth, diffs, base, tend_z, tend_y, tend_x, corr = work[:12]
+    grad, gz, gy, dface, dcell, dline, dline_y = work[12:]
     if mode == "back":
-        prev, own_in, gzlo, gzhi, gylo, gyhi, gxin = take(7)
-    if mode != "back":
-        (state_out,) = take(1)
-    if mode == "fwd":
-        szlo, szhi, sylo, syhi = take(4)
-    if mode == "back":
-        (total,) = take(1)
-    if mode != "fwd":
-        own_out, dzlo, dzhi, dylo, dyhi, dx = take(6)
-    uz, uy, ux, plus, minus, smooth, diffs = take(7)
-    if mode != "back":
-        base, tend_z, tend_y, tend_x, corr = take(5)
-    else:
         base = None
     if mode != "fwd":
-        grad, gz, gy, dface, dcell, dline, dline_y = take(7)
+        dzlo, dzhi, dylo, dyhi = grad_sends
 
     build_lines(scal, q, zlo, zhi, ylo, yhi, xin, uz, uy, ux)
     wants = mode != "back"
@@ -355,9 +338,7 @@
         for c in range(5):
             grad[c] = consts["scale"] * prev[c]
     if mode == "back":
-        gather_grad(
-            prev, consts["coef"], consts["scale"], own_in, gzlo, gzhi, gylo, gyhi, gxin, total, grad
-        )
+        gather_grad(prev, consts["coef"], consts["scale"], own_in, *halo_grad(), total, grad)
     if mode != "fwd":
         grad_faces(grad, gz, gy, dface)
 
@@ -398,13 +379,8 @@
                 consts["first"] * first[c, 0:OWN] + consts["last"] * (q[c, 0:OWN] + t)
             )
             state_out[c, OWN:ROWS] = jnp.ones((ROWS - OWN, LANES), jnp.float32)
-            if mode == "fwd":
-                szlo[c, 0:30] = state_out[c, 0:30]
-                szhi[c, 0:30] = state_out[c, 60:90]
-                for z in range(CZ):
-                    low = z * CY
-                    sylo[c, pl.ds(z, 3, stride=CZ), :] = state_out[c, low : low + 3]
-                    syhi[c, pl.ds(z, 3, stride=CZ), :] = state_out[c, low + 7 : low + 10]
+        if mode == "fwd":
+            cut_edges(state_out, sends)
 
     if mode != "fwd":
         pull_rows("z", dcell, plus, minus, gz, uz, dline)
@@ -416,8 +392,8 @@
         pull_rows("y", dcell, plus, minus, gy, uy, dline_y)
         for c in range(5):
             flip = -1.0 if c == 2 else 1.0
-            dylo[c, 0:27] = dline_y[c, 0:27]
-            dyhi[c, 0:27] = dline_y[c, 117:144]
+            dylo[c, 0:27] = scal[2] * dline_y[c, 0:27]
+            dyhi[c, 0:27] = scal[5] * dline_y[c, 117:144]
             for g in range(3):
                 low = dline_y[c, g * 9 : g * 9 + 9]
                 high = dline_y[c, (13 + g) * 9 : (14 + g) * 9]
@@ -451,49 +427,91 @@
             own_out[c] = acc * lane_mask(ROWS, 3, 125)
 
 
-def finish_kernel(coef, prev, own, zlo, zhi, ylo, yhi, xin, total):
-    gather_grad(prev, coef, None, own, zlo, zhi, ylo, yhi, xin, total, None)
-
-
 FULL = (5, ROWS, LANES)
 EDGE = (5, 32, LANES)
-
-
-def shape(dims):
-    return jax.ShapeDtypeStruct(dims, jnp.float32)
-
-
-def vmem(dims):
-    return pltpu.VMEM(dims, jnp.float32)
-
-
-def section(mode, consts, *args):
-    outs = []
-    if mode != "back":
-        outs.append(FULL)
-    if mode == "fwd":
-        outs += [EDGE] * 4
-    if mode == "back":
-        outs.append(FULL)
-    if mode != "fwd":
-        outs += [FULL] + [EDGE] * 4 + [FULL]
-    line = (5, CELLS, LANES)
-    scratch = [line, line, FULL, line, line, (4, CELLS, LANES), (4, 5, FACES, LANES)]
-    if mode != "back":
-        scratch += [(5, 304, LANES), FULL, FULL, FULL, (5, FACES, LANES)]
-    if mode != "fwd":
-        gpad = (5, GPAD, LANES)
-        scratch += [FULL, gpad, gpad, (5, FACES, LANES), (5, 5, FACES, LANES), line, line]
-    return pl.pallas_call(
-        functools.partial(section_kernel, mode, consts),
-        out_shape=[shape(s) for s in outs],
-        in_specs=[pl.BlockSpec(memory_space=pltpu.SMEM)]
-        + [pl.BlockSpec(memory_space=pltpu.VMEM)] * (len(args) - 1),
-        out_specs=[pl.BlockSpec(memory_space=pltpu.VMEM)] * len(outs),
-        scratch_shapes=[vmem(s) for s in scratch],
-        compiler_params=pltpu.CompilerParams(vmem_limit_bytes=48 * 1024 * 1024),
-        name="section_" + mode,
-    )(*args)
+LINE = (5, CELLS, LANES)
+GLINE = (5, GPAD, LANES)
+WORK = [LINE, LINE, FULL, LINE, LINE, (4, CELLS, LANES), (4, 5, FACES, LANES)]
+WORK += [(5, 304, LANES), FULL, FULL, FULL, (5, FACES, LANES)]
+WORK += [FULL, GLINE, GLINE, (5, FACES, LANES), (5, 5, FACES, LANES), LINE, LINE]
+
+
+def cut_edges(field, sends):
+    szlo, szhi, sylo, syhi = sends
+    for c in range(5):
+        szlo[c, 0:30] = field[c, 0:30]
+        szhi[c, 0:30] = field[c, 60:90]
+        for z in range(CZ):
+            low = z * CY
+            sylo[c, pl.ds(z, 3, stride=CZ), :] = field[c, low : low + 3]
+            syhi[c, pl.ds(z, 3, stride=CZ), :] = field[c, low + 7 : low + 10]
+
+
+def step_kernel(sizes, scal, state, cot, new_out, grad_out, one, two, grad_two, grad_one, own, dx,
+                sends, takes, xtakes, send_sem, recv_sem, *work):
+    peers = []
+    for axis in ("gz", "gy"):
+        place, count = lax.axis_index(axis), sizes[axis]
+        peers.append({axis: lax.rem(place + count - 1, count)})
+        peers.append({axis: lax.rem(place + 1, count)})
+    peers.append({"gx": 1 - lax.axis_index("gx")})
+    mesh_id = pl.DeviceIdType.MESH
+
+    barrier = pltpu.get_barrier_semaphore()
+    for peer in peers:
+        pl.semaphore_signal(barrier, inc=1, device_id=peer, device_id_type=mesh_id)
+    pl.semaphore_wait(barrier, len(peers))
+
+    flights = {}
+
+    def send_to(turn, full):
+        flights[turn] = []
+        for i, peer in enumerate(peers):
+            copy = pltpu.make_async_remote_copy(
+                src_ref=full if i == 4 else sends.at[turn, i],
+                dst_ref=xtakes.at[turn] if i == 4 else takes.at[turn, i ^ 1],
+                send_sem=send_sem.at[turn, i],
+                recv_sem=recv_sem.at[turn, i],
+                device_id=peer,
+                device_id_type=mesh_id,
+            )
+            copy.start()
+            flights[turn].append(copy)
+
+    def arrive(turn):
+        for copy in flights[turn]:
+            copy.wait_recv()
+        return halo(turn)
+
+    def halo(turn):
+        return [takes.at[turn, i] for i in range(4)] + [xtakes.at[turn]]
+
+    def edges(turn):
+        return [sends.at[turn, i] for i in range(4)]
+
+    cut_edges(state, edges(0))
+    send_to(0, state)
+    section("fwd", dict(first=0.0, last=1.0), scal, state, arrive(0), state, None, None, None,
+            one, edges(1), None, None, None, None, work)
+    send_to(1, one)
+    section("fwd", dict(first=0.75, last=0.25), scal, one, arrive(1), state, None, None, None,
+            two, edges(2), None, None, None, None, work)
+    send_to(2, two)
+    section("both", dict(first=1.0 / 3.0, last=2.0 / 3.0, scale=DT * 2.0 / 3.0), scal, two,
+            arrive(2), state, cot, None, None, new_out, None, None, own, edges(3), dx.at[0], work)
+    send_to(3, dx.at[0])
+    section("back", dict(coef=2.0 / 3.0, scale=0.25 * DT), scal, one, halo(1), None, cot, own,
+            lambda: arrive(3), None, None, grad_two, own, edges(4), dx.at[1], work)
+    send_to(4, dx.at[1])
+    section("back", dict(coef=0.25, scale=DT), scal, state, halo(0), None, grad_two, own,
+            lambda: arrive(4), None, None, grad_one, own, edges(5), dx.at[2], work)
+    send_to(5, dx.at[2])
+    for c in range(5):
+        grad_one[c] = grad_one[c] + 0.75 * grad_two[c] + (1.0 / 3.0) * cot[c]
+    gather_grad(grad_one, 1.0, None, own, *arrive(5), grad_out, None)
+    for turn in range(6):
+        for copy in flights[turn]:
+            copy.wait_send()
 
 
 def flat(field, fill):
@@ -507,20 +525,24 @@
     return field[:, :OWN].reshape(5, CZ, CY, LANES)[..., 3 : 3 + CX]
 
 
-def swap(down, up, axis, periodic):
-    count = lax.axis_size(axis)
-    forward = [(i, i + 1) for i in range(count - 1)]
-    if periodic:
-        forward.append((count - 1, 0))
-    backward = [(t, s) for s, t in forward]
-    return lax.ppermute(up, axis, forward), lax.ppermute(down, axis, backward)
-
-
-def exchange(full, zlo, zhi, ylo, yhi):
-    from_z = swap(zlo, zhi, "gz", True)
-    from_y = swap(ylo, yhi, "gy", False)
-    partner = lax.ppermute(full, "gx", [(0, 1), (1, 0)])
-    return (*from_z, *from_y, partner)
+def run_step(scal, state, cot):
+    shape = jax.ShapeDtypeStruct(FULL, jnp.float32)
+    vmem = pl.BlockSpec(memory_space=pltpu.VMEM)
+    scratch = [FULL] * 5 + [(3,) + FULL, (6, 4) + EDGE, (6, 4) + EDGE, (6,) + FULL]
+    sizes = {axis: lax.axis_size(axis) for axis in ("gz", "gy")}
+    return pl.pallas_call(
+        functools.partial(step_kernel, sizes),
+        out_shape=[shape, shape],
+        in_specs=[pl.BlockSpec(memory_space=pltpu.SMEM), vmem, vmem],
+        out_specs=[vmem, vmem],
+        scratch_shapes=[pltpu.VMEM(s, jnp.float32) for s in scratch]
+        + [pltpu.SemaphoreType.DMA((6, 5))] * 2
+        + [pltpu.VMEM(s, jnp.float32) for s in WORK],
+        compiler_params=pltpu.CompilerParams(
+            vmem_limit_bytes=56 * 1024 * 1024, collective_id=0, has_side_effects=True
+        ),
+        name="step",
+    )(scal, state, cot)
 
 
 def on_device(density, momentum, energy, cotangent, bc_codes, weight_in, weight_out):
@@ -540,44 +562,7 @@
     sides = jnp.stack([edges * wall, edges * (1.0 - wall), 1.0 - edges], 1).reshape(12)
     scal = jnp.concatenate([sides, weight_in.reshape(-1), weight_out.reshape(-1)])
 
-    rows = state[:, :OWN].reshape(5, CZ, CY, LANES)
-    tail = lambda v, n: jnp.pad(v.reshape(5, n, LANES), ((0, 0), (0, 32 - n), (0, 0)))
-    by_y = jnp.swapaxes(rows, 1, 2)
-    halo_one = exchange(
-        state,
-        tail(rows[:, 0:3], 30),
-        tail(rows[:, -3:], 30),
-        tail(by_y[:, 0:3], 27),
-        tail(by_y[:, -3:], 27),
-    )
-    one, *edge = section("fwd", dict(first=0.0, last=1.0), scal, state, *halo_one, state)
-    halo_two = exchange(one, *edge)
-    two, *edge = section("fwd", dict(first=0.75, last=0.25), scal, one, *halo_two, state)
-    halo_three = exchange(two, *edge)
-    new_state, own, *edge, dx = section(
-        "both",
-        dict(first=1.0 / 3.0, last=2.0 / 3.0, scale=DT * 2.0 / 3.0),
-        scal,
-        two,
-        *halo_three,
-        state,
-        cot,
-    )
-    back = exchange(dx, *edge)
-    grad_two, own, *edge, dx = section(
-        "back", dict(coef=2.0 / 3.0, scale=0.25 * DT), scal, one, *halo_two, cot, own, *back
-    )
-    back = exchange(dx, *edge)
-    grad_one, own, *edge, dx = section(
-        "back", dict(coef=0.25, scale=DT), scal, state, *halo_one, grad_two, own, *back
-    )
-    back = exchange(dx, *edge)
-    total = pl.pallas_call(
-        functools.partial(finish_kernel, 1.0),
-        out_shape=shape(FULL),
-        name="finish",
-    )(grad_one, own, *back)
-    total = total + 0.75 * grad_two + (1.0 / 3.0) * cot
+    new_state, total = run_step(scal, state, cot)
     return (unflat(new_state), unflat(total))
 
 

time: 178 us -> 132 us (0.74)
  starting transfers between devices: 44.8 us -> 0 us
  waiting for transfers between devices: 26.4 us -> 0 us
  Pallas kernels: 95.2 us -> 120 us
    ppermute x30 -> x0, starting transfers between devices: 44.8 us -> none  [the longest x24 44 us: swap(): return (lax.ppermute(up, axis, forward), lax.ppermute(down, axis, backward))]
    ppermute x30 -> x0, waiting for transfers between devices: 26.4 us -> none  [the longest x24 26.4 us: swap(): return (lax.ppermute(up, axis, forward), lax.ppermute(down, axis, backward))]
    pallas_call x6 -> x1, Pallas kernels: 95.2 us -> 120 us  [run_step(): pl.pallas_call(functools.partial(step_kernel, sizes), out_shape=[shape, s...]
    unnamed x25 -> x7, local copies, waits for them, and re-layouts: 4.05 us -> 1.16 us
  transfers between devices with their start and end apart: 30 -> 0, of which waited for: 13 -> 0; matrix products, arithmetic and copies ran while one was open for 1% -> 0% of each run, Pallas kernels for 0% -> 0%
where the time goes in v1:
time: 132 us
  Pallas kernels  120 us (91%)
  local copies, waits for them, and re-layouts  8.54 us (6%)
  other arithmetic  2.46 us (2%)
    pallas_call x1, Pallas kernels, run_step(): pl.pallas_call(functools.partial(step_kernel, sizes), out_shape=[shape, s...  120 us

profile of v1, /device:TPU:0, one launch (start us, length us, event | category | flops | bytes accessed | tf_op | source)
XLA Modules:
  0.0 131.8 jit_solution(9360207919482234109)
XLA Ops:
  0.6 0.0 copy-start.2
  0.7 0.8 reshape.88
  1.5 0.1 fusion.5
  1.5 0.7 fusion.1
  2.3 0.7 fusion.4
  2.9 0.1 copy.13
  3.0 0.1 reshape.87
  3.1 0.8 copy.14
  3.9 0.1 reshape.89
  4.0 0.6 pad_maximum_fusion.1.scal
  4.6 0.9 copy.15
  5.5 0.9 copy.16
  6.5 0.0 copy-done.2
  6.5 0.4 select_maximum_fusion
  6.9 0.0 copy-start
  6.9 0.7 pad.15.state
  7.6 0.4 copy-done
  8.0 0.2 pad.16
  8.2 0.7 pad.17.cot
  8.9 120.1 %step.1 = (f32[5,96,128]{2,1,0:T(8,128)}, f32[5,96,128]{2,1,0:T(8,128)}) custom-call(f32[108]{0:T(128)} %pad_maximum_fusion.1.scal, f32[5,96,128]{2,1,0:T(8,128)} %pad.15.state, f32[5,96,128]{2,1,0:T(8,128)} %pad.17.cot), custom_call_target="tpu_custom_call" | custom-call | tf_op jit(solution)/shard_map/step/pallas_call | solution.py:533
  129.0 1.0 reshape.93
  129.9 0.0 copy-start.1
  130.0 0.9 slice.17
  130.9 0.0 copy-done.1
  130.9 0.9 slice.16
  (4 shorter events, 0.1 us)
Async XLA Ops:
  0.6 5.8 %copy-start.2 = (f32[3,9,10,122]{3,0,2,1:T(4,128)S(1)}, f32[3,9,10,122]{3,0,2,1:T(4,128)}, u32[]{:S(2)}) copy-start(f32[3,9,10,122]{3,0,2,1:T(4,128)} %param.8) | copy-start | bytes 395284
  6.9 1.1 copy-start
  129.9 0.9 copy-start.1

commit v2 on v1

--- a/solution.py
+++ b/solution.py
@@ -160,7 +160,7 @@
 
 def cell_loop(name, u, plus, minus, smooth, rows):
     def body(i, carry):
-        at = pl.ds(pl.multiple_of(i * 8, 8), 8)
+        at = pl.ds(pl.multiple_of(i * 16, 16), 16)
         cells = [u[c, at, :] for c in range(5)]
         flux, sv = cell_terms(COMP[name], cells)
         for c in range(5):
@@ -171,7 +171,7 @@
                 smooth[c, at, :] = sv[c]
         return carry
 
-    lax.fori_loop(0, rows // 8, body, 0)
+    lax.fori_loop(0, rows // 16, body, 0)
 
 
 def spread_rows(name, plus, minus, diffs, base):
@@ -293,7 +293,7 @@
 
 def pull_cells(name, plus, minus, u, out, rows):
     def body(i, carry):
-        at = pl.ds(pl.multiple_of(i * 8, 8), 8)
+        at = pl.ds(pl.multiple_of(i * 16, 16), 16)
         cells = [u[c, at, :] for c in range(5)]
         dp = [plus[c, at, :] for c in range(5)]
         dm = [minus[c, at, :] for c in range(5)]
@@ -304,7 +304,7 @@
             out[c, at, :] = du[c] + dp[c] - dm[c]
         return carry
 
-    lax.fori_loop(0, rows // 8, body, 0)
+    lax.fori_loop(0, rows // 16, body, 0)
 
 
 def section(mode, consts, scal, q, halo, first, prev, own_in, halo_grad, state_out, sends, total,
@@ -343,7 +343,7 @@
         grad_faces(grad, gz, gy, dface)
 
     def body(i, carry):
-        at = pl.ds(pl.multiple_of(i * 8, 8), 8)
+        at = pl.ds(pl.multiple_of(i * 16, 16), 16)
         d = [[diffs[k, c, at, :] for c in range(5)] for k in range(4)]
         g = None if mode == "fwd" else [dface[c, at, :] for c in range(5)]
         value, cells = weno_unit(d, scal, g, wants)
@@ -356,7 +356,7 @@
                     dcell[k, c, at, :] = cells[k][c]
         return carry
 
-    lax.fori_loop(0, FACES // 8, body, 0)
+    lax.fori_loop(0, FACES // 16, body, 0)
 
     if wants:
         inside = lane_mask(OWN, 3, 125)

time: 132 us -> 120 us (0.909)
  Pallas kernels: 120 us -> 108 us
    pallas_call x1, Pallas kernels: 120 us -> 108 us  [run_step(): pl.pallas_call(functools.partial(step_kernel, sizes), out_shape=[shape, s...]
where the time goes in v2:
time: 120 us; the launch traced here: 119 us
  Pallas kernels  108 us (90%)
  local copies, waits for them, and re-layouts  8.54 us (7%)
  other arithmetic  2.46 us (2%)
    pallas_call x1, Pallas kernels, run_step(): pl.pallas_call(functools.partial(step_kernel, sizes), out_shape=[shape, s...  108 us

profile of v2, /device:TPU:0, one launch (start us, length us, event | category | flops | bytes accessed | tf_op | source)
XLA Modules:
  0.0 119.3 jit_solution(6274110431434644059)
XLA Ops:
  0.6 0.0 copy-start.2
  0.7 0.8 reshape.88
  1.5 0.1 fusion.5
  1.5 0.7 fusion.1
  2.3 0.7 fusion.4
  2.9 0.1 copy.13
  3.0 0.1 reshape.87
  3.1 0.8 copy.14
  3.9 0.1 reshape.89
  4.0 0.6 pad_maximum_fusion.1.scal
  4.6 0.9 copy.15
  5.5 0.9 copy.16
  6.5 0.0 copy-done.2
  6.5 0.4 select_maximum_fusion
  6.9 0.0 copy-start
  6.9 0.7 pad.15.state
  7.6 0.4 copy-done
  8.0 0.2 pad.16
  8.2 0.7 pad.17.cot
  8.9 107.6 %step.1 = (f32[5,96,128]{2,1,0:T(8,128)}, f32[5,96,128]{2,1,0:T(8,128)}) custom-call(f32[108]{0:T(128)} %pad_maximum_fusion.1.scal, f32[5,96,128]{2,1,0:T(8,128)} %pad.15.state, f32[5,96,128]{2,1,0:T(8,128)} %pad.17.cot), custom_call_target="tpu_custom_call" | custom-call | tf_op jit(solution)/shard_map/step/pallas_call | solution.py:533
  116.5 1.0 reshape.93
  117.5 0.0 copy-start.1
  117.5 0.9 slice.17
  118.4 0.0 copy-done.1
  118.4 0.9 slice.16
  (4 shorter events, 0.1 us)
Async XLA Ops:
  0.6 5.8 %copy-start.2 = (f32[3,9,10,122]{3,0,2,1:T(4,128)S(1)}, f32[3,9,10,122]{3,0,2,1:T(4,128)}, u32[]{:S(2)}) copy-start(f32[3,9,10,122]{3,0,2,1:T(4,128)} %param.8) | copy-start | bytes 395284
  6.9 1.1 copy-start
  117.5 0.9 copy-start.1
